TPU v7x, 32 devices: a whole 2x2x4 slice. The times are simulated.
32 devices in a mesh: section: 4 (over y, x), tp: 8 (over z, core).
Axes of the slice: x: 2, y: 2, z: 4, core: 2. Of those that a mesh axis runs over, the one named last changes fastest.
Arguments:
- inputs: bfloat16 [2, 128, 8192], P(None, 'tp'), may hold values from -50 to 50
- cotangent: bfloat16 [2, 128, 8192], P(None, 'tp'), may hold values from -50 to 50
- gains: bfloat16 [4, 8192], P('section'), may hold values from 0.099609375 to 1.8984375
- up_blocks: bfloat16 [4, 18432, 4096], P('section', 'tp'), may hold values from -0.09375 to 0.09375
- up_index: int32 [4, 18432], P('section', 'tp'), may hold values from 0 to 4095, as said below
- up_count: int32 [4, 8], P('section', 'tp'), may hold values from 1792 to 2304, as said below
- down_blocks: bfloat16 [4, 18432, 4096], P('section', 'tp'), may hold values from -0.0625 to 0.0625
- down_index: int32 [4, 18432], P('section', 'tp'), may hold values from 0 to 4095, as said below
- down_count: int32 [4, 8], P('section', 'tp'), may hold values from 1792 to 2304, as said below
Outputs:
- section_outputs: bfloat16 [4, 2, 128, 8192], P('section', None, 'tp')
- input_grads: bfloat16 [4, 2, 128, 8192], P('section', None, 'tp')
- up_grads: bfloat16 [4, 18432, 4096], P('section', 'tp')
- down_grads: bfloat16 [4, 18432, 4096], P('section', 'tp')
Inputs may be any that keep to these rules, and one draw needn't show every extreme that they name: Within one group's 2304 entries of up_index no value repeats. Within one group's 2304 entries of down_index no value repeats. `up_count`: in every layer one group has exactly 2304 live blocks and another exactly 1792. `down_count`: in every layer one group has exactly 2304 live blocks and another exactly 1792.
All inputs are finite; a program needn't handle non-finite values.
Results may differ from a plain program's by a relative error of at most 0.03.
Values may be sent and summed in bfloat16 or wider, within the bound.
No kernel may reach another device: no remote copies, remote signals or barrier semaphores. Data moves between devices by JAX's collectives and lax.ppermute only.
A program may use at most 448 MiB of HBM per device.

v0:
```python
import functools

import jax
import jax.numpy as jnp
from jax import lax
from jax.experimental import pallas as pl
from jax.experimental.pallas import tpu as pltpu
from jax.sharding import PartitionSpec as P

FF = 16384
BLOCK = 64
MICRO = 2
STREAMS = 1
PAIR = 2 * BLOCK
HALF = BLOCK // 2
STRIP = 256
VMEM_BYTES = 58 * 2**20

NORM_EPSILON = 1e-05


def slot_step(slots):
    for size in (192, 128, 64, 32, 16):
        if slots % size == 0:
            return size
    return slots


def split_order(rows_split):
    first = lax.broadcasted_iota(jnp.int32, (STRIP, STRIP), 0)
    second = lax.broadcasted_iota(jnp.int32, (STRIP, STRIP), 1)
    split, natural = (first, second) if rows_split else (second, first)
    inner = split % BLOCK
    target = (split - inner) + 2 * (inner % HALF) + inner // HALF
    return (target == natural).astype(jnp.bfloat16)


def densify_kernel(slots, step_slots, index_ref, count_ref, block_ref, out_ref, held, packed, place):
    step = pl.program_id(0)
    load_steps = slots // step_slots
    width = out_ref.shape[1]
    pairs = width // PAIR
    spare = place.shape[0] - 1

    @pl.when(step == 0)
    def _():
        held[slots] = jnp.zeros((HALF, PAIR), jnp.bfloat16)

        @pl.loop(0, spare // 16)
        def _(group):
            for lane in range(16):
                place[group * 16 + lane] = slots

    @pl.when(step < load_steps)
    def _():
        first = step * step_slots
        for start in range(0, step_slots, 16):
            packed[start : start + 16] = block_ref[start : start + 16, :].reshape(16, HALF, PAIR)
        held[pl.ds(first, step_slots)] = packed[...]

        @pl.loop(0, step_slots // 16)
        def _(group):
            start = pl.multiple_of(group * 16, 16)
            for lane in range(16):
                slot = first + start + lane
                place[jnp.where(slot < count_ref[0], index_ref[slot], spare)] = slot

    @pl.when(step >= load_steps)
    def _():
        strip = step - load_steps
        lane = lax.broadcasted_iota(jnp.int32, (HALF, PAIR), 1)
        low = lane < BLOCK
        for row in range(STRIP // BLOCK):
            for col in range(pairs):
                pair = (strip * (STRIP // BLOCK) + row) * pairs + col
                left = held[place[2 * pair]]
                right = held[place[2 * pair + 1]]
                top = row * BLOCK
                lanes = slice(col * PAIR, (col + 1) * PAIR)
                crossed = pltpu.roll(jnp.where(low, right, left), BLOCK, 1)
                out_ref[top : top + HALF, lanes] = jnp.where(low, left, crossed)
                out_ref[top + HALF : top + BLOCK, lanes] = jnp.where(low, crossed, right)


def densify(blocks, block_index, live_count, row_blocks, col_blocks):
    slots = blocks.shape[0]
    step_slots = slot_step(slots)
    load_steps = slots // step_slots
    width = min(col_blocks * BLOCK, 2048)
    across = col_blocks * BLOCK // width
    strips = row_blocks * BLOCK // STRIP
    if across > 1:
        piece_blocks = width // BLOCK
        row, col = block_index // col_blocks, block_index % col_blocks
        strip, row = row // 4, row % 4
        block_index = ((strip * across + col // piece_blocks) * 4 + row) * piece_blocks + col % piece_blocks

    def out_place(step, index, count):
        spot = jnp.maximum(step - load_steps, 0)
        return (spot // across, spot % across)

    return pl.pallas_call(
        functools.partial(densify_kernel, slots, step_slots),
        grid_spec=pltpu.PrefetchScalarGridSpec(
            num_scalar_prefetch=2,
            grid=(load_steps + strips * across,),
            in_specs=[
                pl.BlockSpec((step_slots, BLOCK * BLOCK), lambda step, index, count: (jnp.minimum(step, load_steps - 1), 0))
            ],
            out_specs=pl.BlockSpec((STRIP, width), out_place),
            scratch_shapes=[
                pltpu.VMEM((slots + 1, HALF, PAIR), jnp.bfloat16),
                pltpu.VMEM((step_slots, HALF, PAIR), jnp.bfloat16),
                pltpu.SMEM((row_blocks * col_blocks + 1,), jnp.int32),
            ],
        ),
        out_shape=jax.ShapeDtypeStruct((row_blocks * BLOCK, col_blocks * BLOCK), jnp.bfloat16),
        compiler_params=pltpu.CompilerParams(
            dimension_semantics=("arbitrary",), vmem_limit_bytes=VMEM_BYTES
        ),
        name="densify",
    )(block_index, live_count, blocks)


def block_grads_kernel(strips, step_slots, index_ref, count_ref, left_ref, right_ref, out_ref, dense, packed):
    step = pl.program_id(0)
    width = right_ref.shape[1]
    pairs = width // PAIR

    @pl.when(step < strips)
    def _():
        left = left_ref[...].T
        high = left.shape[0] // BLOCK
        piece = min(width, 512)

        @pl.loop(0, width // piece)
        def _(number):
            lanes = pl.ds(pl.multiple_of(number * piece, piece), piece)
            product = jnp.dot(left, right_ref[:, lanes], preferred_element_type=jnp.float32).astype(jnp.bfloat16)
            for row in range(high):
                for col in range(piece // PAIR):
                    pair = (step * high + row) * pairs + number * (piece // PAIR) + col
                    cut = slice(col * PAIR, (col + 1) * PAIR)
                    dense[2 * pair] = product[row * BLOCK : row * BLOCK + HALF, cut]
                    dense[2 * pair + 1] = product[row * BLOCK + HALF : (row + 1) * BLOCK, cut]

    @pl.when(step >= strips)
    def _():
        first = (step - strips) * step_slots
        lane = lax.broadcasted_iota(jnp.int32, (HALF, PAIR), 1)
        low = lane < BLOCK

        @pl.loop(0, step_slots // 16)
        def _(group):
            start = pl.multiple_of(group * 16, 16)
            for one in range(16):
                slot = first + start + one
                spot = index_ref[slot]
                keep = dense[spot]
                other = pltpu.roll(dense[spot ^ 1], BLOCK, 1)
                picked = jnp.where(low == (spot % 2 == 0), keep, other)
                packed[one] = jnp.where(slot < count_ref[0], picked, jnp.zeros_like(picked))
            out_ref[pl.ds(start, 16), :] = packed[...].reshape(16, BLOCK * BLOCK)


def block_grads(left, right, block_index, live_count, tokens):
    rows = left.shape[1]
    cols = right.shape[1]
    slots = block_index.shape[0]
    step_slots = slot_step(slots)
    strip = min(rows, 1024 if rows > cols else STRIP)
    strips = rows // strip
    return pl.pallas_call(
        functools.partial(block_grads_kernel, strips, step_slots),
        grid_spec=pltpu.PrefetchScalarGridSpec(
            num_scalar_prefetch=2,
            grid=(strips + slots // step_slots,),
            in_specs=[
                pl.BlockSpec((tokens, strip), lambda step, index, count: (0, jnp.minimum(step, strips - 1))),
                pl.BlockSpec((tokens, cols), lambda step, index, count: (0, 0)),
            ],
            out_specs=pl.BlockSpec(
                (step_slots, BLOCK * BLOCK), lambda step, index, count: (jnp.maximum(step - strips, 0), 0)
            ),
            scratch_shapes=[
                pltpu.VMEM((rows * cols // (HALF * PAIR), HALF, PAIR), jnp.bfloat16),
                pltpu.VMEM((16, HALF, PAIR), jnp.bfloat16),
            ],
        ),
        out_shape=jax.ShapeDtypeStruct((slots, BLOCK * BLOCK), jnp.bfloat16),
        compiler_params=pltpu.CompilerParams(
            dimension_semantics=("arbitrary",), vmem_limit_bytes=VMEM_BYTES
        ),
        cost_estimate=pl.CostEstimate(
            flops=6 * tokens * rows * cols, bytes_accessed=6 * rows * cols, transcendentals=0
        ),
        name="block_grads",
    )(block_index, live_count, left, right)


def normalize(activ_rows, gain):
    values = activ_rows.astype(jnp.float32)
    inv_rms = lax.rsqrt(jnp.mean(values * values, axis=-1, keepdims=True) + NORM_EPSILON)
    return (values, inv_rms, (values * inv_rms * gain.astype(jnp.float32)).astype(jnp.bfloat16))


def same_core():
    count = lax.axis_size("tp")
    return [list(range(core, count, 2)) for core in range(2)]


def other_core(array):
    return lax.ppermute(array, "tp", [(index, index ^ 1) for index in range(lax.axis_size("tp"))])


def all_rows(local_rows):
    return lax.all_gather(local_rows, "tp", axis=0, tiled=True)


def row_sums(part_own, part_other):
    chip = (part_own.astype(jnp.float32) + other_core(part_other).astype(jnp.float32)).astype(jnp.bfloat16)
    return lax.psum_scatter(
        chip, "tp", scatter_dimension=0, tiled=True, axis_index_groups=same_core()
    ).astype(jnp.float32)


def reordered(values, order, dtype=jnp.bfloat16):
    groups = [
        jnp.dot(values[:, start : start + STRIP], order, preferred_element_type=jnp.float32).astype(dtype)
        for start in range(0, values.shape[1], STRIP)
    ]
    return groups[0] if len(groups) == 1 else jnp.concatenate(groups, axis=1)


def reordered_wide(values, order):
    high = values.astype(jnp.bfloat16)
    low = (values - high.astype(jnp.float32)).astype(jnp.bfloat16)
    return reordered(high, order, jnp.float32) + reordered(low, order, jnp.float32)


def times_turned(left, refs):
    transposed = (((1,), (1,)), ((), ()))
    width = refs[0].shape[1]
    total = None
    for number, ref in enumerate(refs):
        part = lax.dot_general(
            left[:, number * width : (number + 1) * width], ref[...], transposed, preferred_element_type=jnp.float32
        )
        total = part if total is None else total + part
    return total


def core_halves(part, local_count, core):
    pieces = [part[start : start + local_count] for start in range(0, part.shape[0], local_count)]
    even = jnp.concatenate(pieces[0::2], axis=0)
    odd = jnp.concatenate(pieces[1::2], axis=0)
    return jnp.where(core == 0, even, odd), jnp.where(core == 0, odd, even)


def forward_kernel(up_steps, turn, base, local_count, flags, rows_ref, *rest):
    ups, downs, rest = rest[:STREAMS], rest[STREAMS : 2 * STREAMS], rest[2 * STREAMS :]
    outs = rest[len(rest) - 8 - turn :]
    part_own, part_other, kept_rows, kept_up, kept_hidden = outs[:5]
    total, order, back = outs[-3:]
    step = pl.program_id(0)
    depth = ups[0].shape[0]
    up_active, down_active, turn_active = flags[base + 0] > 0, flags[base + 1] > 0, flags[base + 3] > 0

    @pl.when(up_active & (step < up_steps))
    def _():
        @pl.when(step == 0)
        def _():
            total[...] = jnp.zeros_like(total)
            order[...] = split_order(False)
            back[...] = split_order(True)

        features = pl.ds(pl.multiple_of(step * depth, depth), depth)
        rows = reordered(rows_ref[:, features], order[...])
        kept_rows[:, features] = rows
        width = ups[0].shape[1]
        for number, ref in enumerate(ups):
            lanes = slice(number * width, (number + 1) * width)
            total[:, lanes] += jnp.dot(rows, ref[...], preferred_element_type=jnp.float32)

        @pl.when(step == up_steps - 1)
        def _():
            proj = total[...]
            kept_up[...] = proj
            gate = 1.0 / (1.0 + jnp.exp(-proj))
            kept_hidden[...] = reordered((proj * gate).astype(jnp.bfloat16), order[...])
            if turn:
                pre_ref, kept_upgrad = rest[0], outs[5]
                act_grad = reordered_wide(pre_ref[...], back[...])
                kept_upgrad[...] = (act_grad * gate * (1.0 + proj * (1.0 - gate))).astype(jnp.bfloat16)

    @pl.when(step >= up_steps)
    def _():
        @pl.when(down_active)
        def _():
            width = downs[0].shape[1]
            hidden = kept_hidden[...]
            for number, ref in enumerate(downs):
                part = jnp.dot(hidden, ref[...], preferred_element_type=jnp.float32).astype(jnp.bfloat16)
                lanes = slice(number * width, (number + 1) * width)
                part_own[:, lanes], part_other[:, lanes] = core_halves(part, local_count, flags[base + 6])

        if turn:

            @pl.when(turn_active)
            def _():
                part = reordered(times_turned(outs[5][...], ups).astype(jnp.bfloat16), back[...])
                part_own[...], part_other[...] = core_halves(part, local_count, flags[base + 6])

        @pl.when(jnp.logical_not(down_active | turn_active))
        def _():
            part_own[...] = jnp.zeros_like(part_own)
            part_other[...] = jnp.zeros_like(part_other)


def layer_cost(tokens, features, units):
    return pl.CostEstimate(flops=4 * tokens * features * units, bytes_accessed=4 * features * units, transcendentals=0)


def forward_layer(flags, base, local_count, rows, w_up, w_down, kept, pre=None):
    turn = pre is not None
    tokens, features = rows.shape
    half = tokens // 2
    units = w_up.shape[1]
    depth = 1024
    up_steps = down_steps = features // depth
    last_up = up_steps - 1
    up_width, down_width = units // STREAMS, depth // STREAMS
    any_space = [pl.BlockSpec(memory_space=pl.ANY)] * len(kept)

    def up_place(number):
        def place(step, flags):
            plain = flags[base + 0] * jnp.minimum(step, last_up)
            return (jnp.where(flags[base + 3] > 0, step % up_steps, plain) if turn else plain, number)

        return place

    def down_place(number):
        return lambda step, flags: (0, STREAMS * flags[base + 1] * jnp.maximum(step - up_steps, 0) + number)

    def part_place(step, flags):
        return (0, jnp.maximum(step - up_steps, 0))

    def kept_place(step, flags):
        return (flags[base + 2], 0)

    pre_spec = [pl.BlockSpec((tokens, units), lambda step, flags: (jnp.minimum(flags[base + 2], MICRO - 1), 0))] * turn
    inputs = [flags, rows, *[w_up] * STREAMS, *[w_down] * STREAMS, *[pre] * turn]
    places = (MICRO + 1) * tokens
    return pl.pallas_call(
        functools.partial(forward_kernel, up_steps, turn, base, local_count),
        grid_spec=pltpu.PrefetchScalarGridSpec(
            num_scalar_prefetch=1,
            grid=(up_steps + down_steps,),
            in_specs=[pl.BlockSpec((tokens, features), lambda step, flags: (0, 0))]
            + [pl.BlockSpec((depth, up_width), up_place(number)) for number in range(STREAMS)]
            + [pl.BlockSpec((units, down_width), down_place(number)) for number in range(STREAMS)]
            + pre_spec
            + any_space,
            out_specs=[pl.BlockSpec((half, depth), part_place)] * 2
            + [
                pl.BlockSpec((tokens, features), kept_place),
                pl.BlockSpec((tokens, units), kept_place),
                pl.BlockSpec((tokens, units), kept_place),
            ]
            + [pl.BlockSpec((tokens, units), kept_place)] * turn,
            scratch_shapes=[
                pltpu.VMEM((tokens, units), jnp.float32),
                pltpu.VMEM((STRIP, STRIP), jnp.bfloat16),
                pltpu.VMEM((STRIP, STRIP), jnp.bfloat16),
            ],
        ),
        out_shape=[jax.ShapeDtypeStruct((half, features), jnp.bfloat16)] * 2
        + [
            jax.ShapeDtypeStruct((places, features), jnp.bfloat16),
            jax.ShapeDtypeStruct((places, units), jnp.float32),
            jax.ShapeDtypeStruct((places, units), jnp.bfloat16),
        ]
        + [jax.ShapeDtypeStruct((places, units), jnp.bfloat16)] * turn,
        input_output_aliases={len(inputs) + number: 2 + number for number in range(len(kept))},
        compiler_params=pltpu.CompilerParams(dimension_semantics=("arbitrary",), vmem_limit_bytes=VMEM_BYTES),
        cost_estimate=layer_cost(tokens, features, units),
        name="forward_layer",
    )(*inputs, *kept)


def backward_kernel(down_steps, base, local_count, flags, grad_ref, proj_ref, *rest):
    downs, ups = rest[:STREAMS], rest[STREAMS : 2 * STREAMS]
    part_own, part_other, kept_grad, kept_upgrad, back = rest[-5:]
    step = pl.program_id(0)
    width = downs[0].shape[0]
    active = flags[base + 4] > 0

    @pl.when(active & (step < down_steps))
    def _():
        @pl.when(step == 0)
        def _():
            kept_grad[...] = grad_ref[...]
            back[...] = split_order(True)

        act_grad = reordered_wide(times_turned(grad_ref, downs), back[...])
        lanes = pl.ds(pl.multiple_of(step * width, width), width)
        proj = proj_ref[:, lanes]
        gate = 1.0 / (1.0 + jnp.exp(-proj))
        kept_upgrad[:, lanes] = (act_grad * gate * (1.0 + proj * (1.0 - gate))).astype(jnp.bfloat16)

    @pl.when(step >= down_steps)
    def _():
        @pl.when(active)
        def _():
            part = reordered(times_turned(kept_upgrad[...], ups).astype(jnp.bfloat16), back[...])
            part_own[...], part_other[...] = core_halves(part, local_count, flags[base + 6])

        @pl.when(jnp.logical_not(active))
        def _():
            part_own[...] = jnp.zeros_like(part_own)
            part_other[...] = jnp.zeros_like(part_other)


def backward_layer(flags, base, local_count, grad, kept_up, w_up, w_down, kept):
    tokens, features = grad.shape
    half = tokens // 2
    units = w_up.shape[1]
    width, depth = min(units, STRIP), 1024
    down_steps, up_steps = units // width, features // depth
    last_down = down_steps - 1
    any_space = [pl.BlockSpec(memory_space=pl.ANY)] * len(kept)

    def down_place(number):
        return lambda step, flags: (flags[base + 4] * jnp.minimum(step, last_down), number)

    def up_place(number):
        return lambda step, flags: (flags[base + 4] * jnp.maximum(step - down_steps, 0), number)

    def part_place(step, flags):
        return (0, jnp.maximum(step - down_steps, 0))

    def kept_place(step, flags):
        return (flags[base + 5], 0)

    inputs = [flags, grad, kept_up, *[w_down] * STREAMS, *[w_up] * STREAMS]
    places = (MICRO + 1) * tokens
    return pl.pallas_call(
        functools.partial(backward_kernel, down_steps, base, local_count),
        grid_spec=pltpu.PrefetchScalarGridSpec(
            num_scalar_prefetch=1,
            grid=(down_steps + up_steps,),
            in_specs=[pl.BlockSpec((tokens, features), lambda step, flags: (0, 0))]
            + [pl.BlockSpec((tokens, units), kept_place)]
            + [pl.BlockSpec((width, features // STREAMS), down_place(number)) for number in range(STREAMS)]
            + [pl.BlockSpec((depth, units // STREAMS), up_place(number)) for number in range(STREAMS)]
            + any_space,
            out_specs=[pl.BlockSpec((half, depth), part_place)] * 2
            + [pl.BlockSpec((tokens, features), kept_place), pl.BlockSpec((tokens, units), kept_place)],
            scratch_shapes=[pltpu.VMEM((STRIP, STRIP), jnp.bfloat16)],
        ),
        out_shape=[jax.ShapeDtypeStruct((half, features), jnp.bfloat16)] * 2
        + [
            jax.ShapeDtypeStruct((places, features), jnp.bfloat16),
            jax.ShapeDtypeStruct((places, units), jnp.bfloat16),
        ],
        input_output_aliases={len(inputs) + number: 2 + number for number in range(len(kept))},
        compiler_params=pltpu.CompilerParams(dimension_semantics=("arbitrary",), vmem_limit_bytes=VMEM_BYTES),
        cost_estimate=layer_cost(tokens, features, units),
        name="backward_layer",
    )(*inputs, *kept)


def put(buffer, value, place):
    return lax.dynamic_update_slice_in_dim(buffer, value, place * value.shape[0], 0)


def take(buffer, place, count):
    return lax.dynamic_slice_in_dim(buffer, place * count, count, 0)


def shards(
    inputs, cotangent, gains, up_blocks, up_index, up_count, down_blocks, down_index, down_count
):
    micro_count, tok_rows, features = inputs.shape
    section_index = lax.axis_index("section")
    section_count = lax.axis_size("section")
    last = section_count - 1
    tp_count = lax.axis_size("tp")
    group_width = FF // tp_count
    total_rows = tok_rows * tp_count
    row_blocks = features // BLOCK
    group_blocks = group_width // BLOCK
    gain = gains[0]
    gathered = all_rows(normalize(inputs[0], gain)[2])
    cot_rows = [all_rows(cotangent[micro]) for micro in range(micro_count)]
    w_up = densify(up_blocks[0], up_index[0], up_count[0], row_blocks, group_blocks)
    w_down = densify(down_blocks[0], down_index[0], down_count[0], group_blocks, row_blocks)
    gathered, cot_rows, w_up, w_down = lax.optimization_barrier((gathered, cot_rows, w_up, w_down))
    live_rows = micro_count * total_rows

    places = micro_count + 1
    kept_fwd = []
    kept_input = jnp.zeros((places * tok_rows, features), jnp.bfloat16)
    kept_output = jnp.zeros((places * tok_rows, features), jnp.bfloat16)
    kept_ingrad = jnp.zeros((places * tok_rows, features), jnp.bfloat16)
    is_last = section_index == last

    rounds = 2 * section_count - 1
    ticks = rounds + micro_count - 1
    current = inputs[0]
    table = []
    for tick in range(ticks):
        micro_fwd = tick - section_index
        micro_bwd = tick - (2 * last - section_index)
        fwd_active = (micro_fwd >= 0) & (micro_fwd < micro_count)
        bwd_active = (micro_bwd >= 0) & (micro_bwd < micro_count) & jnp.logical_not(is_last)
        table += [
            fwd_active,
            fwd_active & jnp.logical_not(is_last),
            jnp.where(fwd_active, micro_fwd, micro_count),
            fwd_active & is_last,
            bwd_active,
            jnp.where(bwd_active, micro_bwd, micro_count),
            lax.axis_index("tp") % 2,
        ]
    flags = jnp.stack([jnp.asarray(entry, jnp.int32) for entry in table])
    flags, gathered = lax.optimization_barrier((flags, gathered))
    for tick in range(ticks):
        base = 7 * tick
        micro_fwd = tick - section_index
        micro_bwd = tick - (2 * last - section_index)
        fwd_active = (micro_fwd >= 0) & (micro_fwd < micro_count)
        bwd_active = (micro_bwd >= 0) & (micro_bwd < micro_count)
        any_fwd = tick <= last + micro_count - 1
        any_bwd = tick >= last
        partial = None
        if tick + 1 == ticks:
            final, gathered = lax.optimization_barrier((final, gathered))
            final_sums = lax.psum_scatter(final, "tp", scatter_dimension=0, tiled=True).astype(jnp.float32)
        if any_fwd:
            place = jnp.where(fwd_active, micro_fwd, micro_count)
            if tick < last:
                *partial, kept_rows, kept_up, kept_hidden = forward_layer(
                    flags, base, tok_rows, gathered, w_up, w_down, kept_fwd
                )
                kept_fwd = [kept_rows, kept_up, kept_hidden]
            else:
                *partial, kept_rows, kept_up, kept_hidden, kept_upgrad = forward_layer(
                    flags, base, tok_rows, gathered, w_up, w_down, kept_fwd, pre_grad
                )
                kept_fwd = [kept_rows, kept_up, kept_hidden, kept_upgrad]
            kept_input = put(kept_input, current, place)
        if tick == 0:
            cot_rows, partial = lax.optimization_barrier((cot_rows, partial))
            kept_grad = jnp.concatenate(cot_rows + [jnp.zeros((total_rows, features), jnp.bfloat16)])
        if tick == 1:
            cot_all, partial = lax.optimization_barrier((kept_grad, partial))
            pre_grad = lax.cond(
                is_last,
                lambda: jnp.dot(cot_all[:live_rows], w_down.T, preferred_element_type=jnp.float32),
                lambda: jnp.zeros((live_rows, group_width), jnp.float32),
            )
        if any_bwd:
            place_bwd = jnp.where(bwd_active, micro_bwd, micro_count)
            incoming = current
            if tick - last < micro_count:
                incoming = jnp.where(is_last, cotangent[tick - last], current)
        if tick > last:
            *back, kept_grad, kept_upgrad = backward_layer(
                flags, base, tok_rows, gathered, kept_up, w_up, w_down, [kept_grad, kept_upgrad]
            )
            if any_fwd:
                back = [jnp.where(is_last, turned, one) for turned, one in zip(partial, back)]
            partial = back
        if tick == last + micro_count:
            hidden, partial = lax.optimization_barrier((kept_hidden, partial))

            def last_sums():
                parts = jnp.dot(hidden[:live_rows], w_down, preferred_element_type=jnp.float32).astype(jnp.bfloat16)
                parts = parts.reshape(micro_count, tp_count, tok_rows, features)
                return parts.swapaxes(0, 1).reshape(live_rows, features)

            final = lax.cond(is_last, last_sums, lambda: jnp.zeros((live_rows, features), jnp.bfloat16))
        sums = row_sums(*partial)
        if tick == 1:
            pre_grad, sums = lax.optimization_barrier((pre_grad, sums))
        if tick == last + micro_count:
            final, sums = lax.optimization_barrier((final, sums))
        if tick + 1 == ticks:
            up_grads = block_grads(kept_rows, kept_upgrad, up_index[0], up_count[0], live_rows)
            sums, up_grads = lax.optimization_barrier((sums, up_grads))
        send = None
        if any_fwd and tick < last + micro_count - 1:
            layer_out = (current.astype(jnp.float32) + sums).astype(jnp.bfloat16)
            kept_output = put(kept_output, layer_out, place)
            send = layer_out
        if any_bwd:
            values, inv_rms, _ = normalize(take(kept_input, place_bwd, tok_rows), gain)
            scaled_grad = sums * gain.astype(jnp.float32)
            norm_term = inv_rms * scaled_grad - values * (inv_rms * inv_rms * inv_rms) * jnp.mean(
                scaled_grad * values, axis=-1, keepdims=True
            )
            grad_in = (incoming.astype(jnp.float32) + norm_term).astype(jnp.bfloat16)
            kept_ingrad = put(kept_ingrad, grad_in, place_bwd)
            send = grad_in if send is None else jnp.where(bwd_active, grad_in, send)
        if tick + 1 == ticks:
            break
        pairs = []
        for micro in range(micro_count):
            done = tick - micro
            if 0 <= done < rounds - 1:
                pairs.append((last - abs(last - done), last - abs(last - done - 1)))
        current = lax.ppermute(send, "section", pairs)
        if tick + 1 < micro_count:
            current = jnp.where(section_index == 0, inputs[tick + 1], current)
        next_fwd = tick + 1 <= last + micro_count - 1
        next_bwd = tick + 1 > last
        source = current
        if next_fwd:
            source = normalize(current, gain)[2]
            if next_bwd:
                source = jnp.where(section_index + micro_count > tick + 1, source, current)
        gathered = all_rows(source)

    down_grads = block_grads(kept_hidden, kept_grad, down_index[0], down_count[0], live_rows)
    final_out = (kept_input[: micro_count * tok_rows].astype(jnp.float32) + final_sums).astype(jnp.bfloat16)
    outputs = jnp.where(is_last, final_out, kept_output[: micro_count * tok_rows])
    shape = (1, micro_count, tok_rows, features)
    return (
        outputs.reshape(shape),
        kept_ingrad[: micro_count * tok_rows].reshape(shape),
        up_grads[None],
        down_grads[None],
    )


def solution(mesh):
    return jax.shard_map(
        shards,
        mesh=mesh,
        in_specs=(
            P(None, "tp", None),
            P(None, "tp", None),
            P("section", None),
            P("section", "tp", None),
            P("section", "tp"),
            P("section", "tp"),
            P("section", "tp", None),
            P("section", "tp"),
            P("section", "tp"),
        ),
        out_specs=(
            P("section", None, "tp", None),
            P("section", None, "tp", None),
            P("section", "tp", None),
            P("section", "tp", None),
        ),
        check_vma=False,
    )
```

profile of v0, /device:TPU:0, one launch (start us, length us, event | category | flops | bytes accessed | tf_op | source)
XLA Modules:
  0.0 1020.3 jit_solution(4046073839510620570)
XLA Ops:
  16.5 41.0 %densify.3.rest_1_.rest_0_ = bf16[2048,8192]{1,0:T(8,128)(2,1)} custom-call(s32[2304]{0:T(1024)} %fusion.62.index_ref, s32[1]{0:T(128)} %bitcast.87.count_ref, bf16[2304,4096]{1,0:T(8,128)(2,1)} %bitcast.89), custom_call_target="tpu_custom_call" | custom-call | tf_op jit(solution)/shard_map/densify/pallas_call | solution.py:102
  57.5 40.9 %densify.2.rest_0_.rest_1_ = bf16[8192,2048]{1,0:T(8,128)(2,1)} custom-call(s32[2304]{0:T(1024)} %reduce.index_ref, s32[1]{0:T(128)} %bitcast.85.count_ref, bf16[2304,4096]{1,0:T(8,128)(2,1)} %bitcast.90), custom_call_target="tpu_custom_call" | custom-call | tf_op jit(solution)/shard_map/densify/pallas_call | solution.py:102
  99.1 5.4 all-gather.29.cloned.1.call-done
  104.5 31.7 %forward_layer.5 = (bf16[64,8192]{1,0:T(8,128)(2,1)}, bf16[64,8192]{1,0:T(8,128)(2,1)}, bf16[384,8192]{1,0:T(8,128)(2,1)}, f32[384,2048]{1,0:T(8,128)}, bf16[384,2048]{1,0:T(8,128)(2,1)S(1)}) custom-call(s32[56]{0:T(128)} %stack.334.flags, bf16[128,8192]{1,0:T(8,128)(2,1)} %all-gather.13.cloned.1.call-done.rows_ref, ...), custom_call_target="tpu_custom_call" | custom-call | flops 8589934592 | bytes 67108864 | tf_op jit(solution)/shard_map/forward_layer/pallas_call | solution.py:354
  141.7 24.9 %reduce-scatter.10.cloned.1.call-done = bf16[16,8192]{1,0:T(8,128)(2,1)} async-done(((bf16[64,8192]{1,0:T(8,128)(2,1)}), bf16[16,8192]{1,0:T(8,128)(2,1)}) %reduce-scatter.10.cloned.1.call-update) | async-done | bytes 262160 | tf_op jit(solution)/shard_map/reduce_scatter | solution.py:222
  172.2 5.3 collective-permute-done.1
  178.7 6.1 maximum_maximum_fusion.rest_2_
  184.8 22.0 %all-gather.15.cloned.1.call-done.rows_ref = bf16[128,8192]{1,0:T(8,128)(2,1)} async-done(((bf16[16,8192]{1,0:T(8,128)(2,1)}), bf16[128,8192]{1,0:T(8,128)(2,1)}) %all-gather.15.cloned.1.call-update) | async-done | bytes 2097168 | tf_op jit(solution)/shard_map/all_gather | solution.py:217
  206.8 31.7 %forward_layer.6 = (bf16[64,8192]{1,0:T(8,128)(2,1)}, bf16[64,8192]{1,0:T(8,128)(2,1)}, bf16[384,8192]{1,0:T(8,128)(2,1)}, f32[384,2048]{1,0:T(8,128)}, bf16[384,2048]{1,0:T(8,128)(2,1)S(1)}) custom-call(s32[56]{0:T(128)} %stack.334.flags, ...), custom_call_target="tpu_custom_call", output_to_operand_aliasing={{2}: (4, {}), {3}: (5, {}), {4}: (6, {})} | custom-call | flops 8589934592 | bytes 67108864 | tf_op jit(solution)/shard_map/forward_layer/pallas_call | solution.py:354
  245.6 24.2 %reduce-scatter.12.cloned.1.call-done = bf16[16,8192]{1,0:T(8,128)(2,1)} async-done(((bf16[64,8192]{1,0:T(8,128)(2,1)}), bf16[16,8192]{1,0:T(8,128)(2,1)}) %reduce-scatter.12.cloned.1.call-update) | async-done | bytes 262160 | tf_op jit(solution)/shard_map/reduce_scatter | solution.py:222
  280.8 29.1 %all-gather.17.cloned.1.call-done.rows_ref = bf16[128,8192]{1,0:T(8,128)(2,1)} async-done(((bf16[16,8192]{1,0:T(8,128)(2,1)}), bf16[128,8192]{1,0:T(8,128)(2,1)}) %all-gather.17.cloned.1.call-update) | async-done | bytes 2097168 | tf_op jit(solution)/shard_map/all_gather | solution.py:217
  309.8 8.9 forward_layer.7
  324.2 48.7 %reduce-scatter.14.cloned.1.call-done = bf16[16,8192]{1,0:T(8,128)(2,1)} async-done(((bf16[64,8192]{1,0:T(8,128)(2,1)}), bf16[16,8192]{1,0:T(8,128)(2,1)}) %reduce-scatter.14.cloned.1.call-update) | async-done | bytes 262160 | tf_op jit(solution)/shard_map/reduce_scatter | solution.py:222
  375.7 37.1 %all-gather.19.cloned.1.call-done.rows_ref = bf16[128,8192]{1,0:T(8,128)(2,1)} async-done(((bf16[16,8192]{1,0:T(8,128)(2,1)}), bf16[128,8192]{1,0:T(8,128)(2,1)}) %all-gather.19.cloned.1.call-update) | async-done | bytes 2097168 | tf_op jit(solution)/shard_map/all_gather | solution.py:217
  412.8 9.4 forward_layer.8
  427.8 53.2 %reduce-scatter.16.cloned.1.call-done = bf16[16,8192]{1,0:T(8,128)(2,1)} async-done(((bf16[64,8192]{1,0:T(8,128)(2,1)}), bf16[16,8192]{1,0:T(8,128)(2,1)}) %reduce-scatter.16.cloned.1.call-update) | async-done | bytes 262160 | tf_op jit(solution)/shard_map/reduce_scatter | solution.py:222
  486.5 37.1 %all-gather.21.cloned.1.call-done.rows_ref.grad_ref = bf16[128,8192]{1,0:T(8,128)(2,1)} async-done(((bf16[16,8192]{1,0:T(8,128)(2,1)}), bf16[128,8192]{1,0:T(8,128)(2,1)}) %all-gather.21.cloned.1.call-update) | async-done | bytes 2097168 | tf_op jit(solution)/shard_map/all_gather | solution.py:217
  523.6 9.4 forward_layer.9
  533.1 9.1 backward_layer.4
  547.9 54.9 %reduce-scatter.18.cloned.1.call-done = bf16[16,8192]{1,0:T(8,128)(2,1)} async-done(((bf16[64,8192]{1,0:T(8,128)(2,1)}), bf16[16,8192]{1,0:T(8,128)(2,1)}) %reduce-scatter.18.cloned.1.call-update) | async-done | bytes 262160 | tf_op jit(solution)/shard_map/reduce_scatter | solution.py:222
  607.0 37.1 %all-gather.23.cloned.1.call-done.grad_ref = bf16[128,8192]{1,0:T(8,128)(2,1)} async-done(((bf16[16,8192]{1,0:T(8,128)(2,1)}), bf16[128,8192]{1,0:T(8,128)(2,1)}) %all-gather.23.cloned.1.call-update) | async-done | bytes 2097168 | tf_op jit(solution)/shard_map/all_gather | solution.py:217
  644.1 9.0 backward_layer.5
  661.4 52.2 %reduce-scatter.20.cloned.1.call-done = bf16[16,8192]{1,0:T(8,128)(2,1)} async-done(((bf16[64,8192]{1,0:T(8,128)(2,1)}), bf16[16,8192]{1,0:T(8,128)(2,1)}) %reduce-scatter.20.cloned.1.call-update) | async-done | bytes 262160 | tf_op jit(solution)/shard_map/reduce_scatter | solution.py:222
  716.3 8.5 collective-permute-done.11
  725.6 28.0 %all-gather.25.cloned.1.call-done.grad_ref = bf16[128,8192]{1,0:T(8,128)(2,1)} async-done(((bf16[16,8192]{1,0:T(8,128)(2,1)}), bf16[128,8192]{1,0:T(8,128)(2,1)}) %all-gather.25.cloned.1.call-update) | async-done | bytes 2097168 | tf_op jit(solution)/shard_map/all_gather | solution.py:217
  753.6 38.2 %backward_layer.6 = (bf16[64,8192]{1,0:T(8,128)(2,1)}, bf16[64,8192]{1,0:T(8,128)(2,1)}, bf16[384,8192]{1,0:T(8,128)(2,1)}, bf16[384,2048]{1,0:T(8,128)(2,1)}) custom-call(s32[56]{0:T(128)} %stack.334.flags, bf16[128,8192]{1,0:T(8,128)(2,1)} %all-gather.25.cloned.1.call-done.grad_ref, ...), custom_call_target="tpu_custom_call", output_to_operand_aliasing={{2}: (5, {}), {3}: (6, {})} | custom-call | flops 8589934592 | bytes 67108864 | tf_op jit(solution)/shard_map/backward_layer/pallas_call | solution.py:447
  797.4 25.8 %reduce-scatter.22.cloned.1.call-done = bf16[16,8192]{1,0:T(8,128)(2,1)} async-done(((bf16[64,8192]{1,0:T(8,128)(2,1)}), bf16[16,8192]{1,0:T(8,128)(2,1)}) %reduce-scatter.22.cloned.1.call-update) | async-done | bytes 262160 | tf_op jit(solution)/shard_map/reduce_scatter | solution.py:222
  826.9 8.5 collective-permute-done.13
  836.1 26.3 %all-gather.27.cloned.1.call-done.grad_ref = bf16[128,8192]{1,0:T(8,128)(2,1)} async-done(((bf16[16,8192]{1,0:T(8,128)(2,1)}), bf16[128,8192]{1,0:T(8,128)(2,1)}) %all-gather.27.cloned.1.call-update) | async-done | bytes 2097168 | tf_op jit(solution)/shard_map/all_gather | solution.py:217
  862.4 38.3 %backward_layer.7 = (bf16[64,8192]{1,0:T(8,128)(2,1)}, bf16[64,8192]{1,0:T(8,128)(2,1)}, bf16[384,8192]{1,0:T(8,128)(2,1)}, bf16[384,2048]{1,0:T(8,128)(2,1)}) custom-call(s32[56]{0:T(128)} %stack.334.flags, bf16[128,8192]{1,0:T(8,128)(2,1)} %all-gather.27.cloned.1.call-done.grad_ref, ...), custom_call_target="tpu_custom_call", output_to_operand_aliasing={{2}: (5, {}), {3}: (6, {})} | custom-call | flops 8589934592 | bytes 67108864 | tf_op jit(solution)/shard_map/backward_layer/pallas_call | solution.py:447
  906.8 59.0 %block_grads.3 = bf16[2304,4096]{1,0:T(8,128)(2,1)} custom-call(s32[2304]{0:T(1024)} %copy-done.15, s32[1]{0:T(128)} %bitcast.88.count_ref, bf16[384,2048]{1,0:T(8,128)(2,1)S(1)} %get-tuple-element.138.left_ref, bf16[384,8192]{1,0:T(8,128)(2,1)} %get-tuple-element.157.right_ref), custom_call_target="tpu_custom_call" | custom-call | flops 25769803776 | bytes 100663296 | tf_op jit(solution)/shard_map/block_grads/pallas_call | solution.py:173
  965.8 43.2 %block_grads.2 = bf16[2304,4096]{1,0:T(8,128)(2,1)} custom-call(s32[2304]{0:T(1024)} %reduce.index_ref, s32[1]{0:T(128)} %bitcast.86.count_ref, bf16[384,8192]{1,0:T(8,128)(2,1)} %get-tuple-element.153.left_ref, bf16[384,2048]{1,0:T(8,128)(2,1)} %get-tuple-element.154.right_ref), custom_call_target="tpu_custom_call" | custom-call | flops 25769803776 | bytes 100663296 | tf_op jit(solution)/shard_map/block_grads/pallas_call | solution.py:173
  (175 shorter events, 103.5 us)
Async XLA Ops:
  7.2 91.9 %all-gather.13.cloned.1.call-start = ((), (), s32[]{:S(2)}) async-start(), calls=%async_computation.9 | async-start | bytes 2359296 | tf_op jit(solution)/shard_map/all_gather | solution.py:217
  11.0 88.1 %all-gather.31.cloned.1.call-start = ((), (), s32[]{:S(2)}) async-start(), calls=%async_computation.27 | async-start | bytes 2359296 | tf_op jit(solution)/shard_map/all_gather | solution.py:217
  12.9 91.6 %all-gather.29.cloned.1.call-start = ((), (), s32[]{:S(2)}) async-start(), calls=%async_computation.26 | async-start | bytes 2359296 | tf_op jit(solution)/shard_map/all_gather | solution.py:217
  13.6 153.0 %reduce-scatter.10.cloned.1.call-start = ((), (), s32[]{:S(2)}) async-start(), calls=%async_computation.10 | async-start | bytes 1310720 | tf_op jit(solution)/shard_map/reduce_scatter | solution.py:222
  136.3 2.9 collective-permute-start
  141.7 65.1 %all-gather.15.cloned.1.call-start = ((), (), s32[]{:S(2)}) async-start(), calls=%async_computation.11 | async-start | bytes 2359296 | tf_op jit(solution)/shard_map/all_gather | solution.py:217
  168.7 8.7 collective-permute-start.1
  178.6 91.2 %reduce-scatter.12.cloned.1.call-start = ((), (), s32[]{:S(2)}) async-start(), calls=%async_computation.12 | async-start | bytes 1310720 | tf_op jit(solution)/shard_map/reduce_scatter | solution.py:222
  238.5 2.9 collective-permute-start.2
  243.9 65.9 %all-gather.17.cloned.1.call-start = ((), (), s32[]{:S(2)}) async-start(), calls=%async_computation.13 | async-start | bytes 2359296 | tf_op jit(solution)/shard_map/all_gather | solution.py:217
  270.9 8.8 collective-permute-start.3
  280.7 92.2 %reduce-scatter.14.cloned.1.call-start = ((), (), s32[]{:S(2)}) async-start(), calls=%async_computation.14 | async-start | bytes 1310720 | tf_op jit(solution)/shard_map/reduce_scatter | solution.py:222
  318.7 2.9 collective-permute-start.4
  324.1 88.7 %all-gather.19.cloned.1.call-start = ((), (), s32[]{:S(2)}) async-start(), calls=%async_computation.15 | async-start | bytes 2359296 | tf_op jit(solution)/shard_map/all_gather | solution.py:217
  373.9 0.7 collective-permute-start.5
  375.7 105.3 %reduce-scatter.16.cloned.1.call-start = ((), (), s32[]{:S(2)}) async-start(), calls=%async_computation.16 | async-start | bytes 1310720 | tf_op jit(solution)/shard_map/reduce_scatter | solution.py:222
  422.3 2.9 collective-permute-start.6
  427.7 95.9 %all-gather.21.cloned.1.call-start = ((), (), s32[]{:S(2)}) async-start(), calls=%async_computation.17 | async-start | bytes 2359296 | tf_op jit(solution)/shard_map/all_gather | solution.py:217
  486.2 116.6 %reduce-scatter.18.cloned.1.call-start = ((), (), s32[]{:S(2)}) async-start(), calls=%async_computation.18 | async-start | bytes 1310720 | tf_op jit(solution)/shard_map/reduce_scatter | solution.py:222
  543.7 2.7 collective-permute-start.8
  547.8 96.3 %all-gather.23.cloned.1.call-start = ((), (), s32[]{:S(2)}) async-start(), calls=%async_computation.19 | async-start | bytes 2359296 | tf_op jit(solution)/shard_map/all_gather | solution.py:217
  607.0 106.6 %reduce-scatter.20.cloned.1.call-start = ((), (), s32[]{:S(2)}) async-start(), calls=%async_computation.20 | async-start | bytes 1310720 | tf_op jit(solution)/shard_map/reduce_scatter | solution.py:222
  653.2 2.9 collective-permute-start.10
  658.6 95.0 %all-gather.25.cloned.1.call-start = ((), (), s32[]{:S(2)}) async-start(), calls=%async_computation.21 | async-start | bytes 2359296 | tf_op jit(solution)/shard_map/all_gather | solution.py:217
  715.0 9.8 collective-permute-start.11
  725.6 97.7 %reduce-scatter.22.cloned.1.call-start = ((), (), s32[]{:S(2)}) async-start(), calls=%async_computation.22 | async-start | bytes 1310720 | tf_op jit(solution)/shard_map/reduce_scatter | solution.py:222
  791.9 2.9 collective-permute-start.12
  797.3 65.0 %all-gather.27.cloned.1.call-start = ((), (), s32[]{:S(2)}) async-start(), calls=%async_computation.23 | async-start | bytes 2359296 | tf_op jit(solution)/shard_map/all_gather | solution.py:217
  825.6 9.8 collective-permute-start.13
  836.1 172.9 %reduce-scatter.26.cloned.1.call-start = ((), (), s32[]{:S(2)}) async-start(), calls=%async_computation.25 | async-start | bytes 1310720 | tf_op jit(solution)/shard_map/reduce_scatter | solution.py:222
  900.6 2.9 collective-permute-start.14
  906.1 105.2 %reduce-scatter.24.cloned.1.call-start = ((), (), s32[]{:S(2)}) async-start(), calls=%async_computation.24 | async-start | bytes 4718592 | tf_op jit(solution)/shard_map/reduce_scatter | solution.py:539
  (20 other events, 321.1 us)
Sparse Core Ops, SparseCore 0:
  11.1 31.7 all-gather.12
  45.1 28.5 all-gather.30
  75.9 28.5 all-gather.28
  141.8 24.8 reduce-scatter.9
  178.7 28.0 all-gather.14
  244.1 25.6 reduce-scatter.11
  280.8 28.9 all-gather.16
  324.3 48.5 reduce-scatter.13
  375.8 37.0 all-gather.18
  427.8 53.0 reduce-scatter.15
  486.4 37.2 all-gather.20
  548.0 54.8 reduce-scatter.17
  607.1 37.0 all-gather.22
  658.8 54.8 reduce-scatter.19
  725.7 27.9 all-gather.24
  797.5 25.7 reduce-scatter.21
  836.2 26.1 all-gather.26
  906.2 24.8 reduce-scatter.25
  933.4 48.6 reduce-scatter.23
where the time goes:
time: 1030 us; the launch traced here: 1020 us
  waiting for transfers between devices  556 us (54%)
  Pallas kernels  370 us (36%)
  other arithmetic  52 us (5%)
  between operations  16.4 us (2%)
  starting transfers between devices  14.9 us (1%)
  local copies, waits for them, and re-layouts  10.7 us (1%)
    reduce_scatter x8, waiting for transfers between devices, row_sums(): lax.psum_scatter(chip, 'tp', scatter_dimension=0, tiled=True, axis_index_...  284 us
    all_gather x10, waiting for transfers between devices, all_rows(): return lax.all_gather(local_rows, 'tp', axis=0, tiled=True)  222 us
    pallas_call x2, Pallas kernels, block_grads(): pl.pallas_call(functools.partial(block_grads_kernel, strips, step_slots),...  102 us
    pallas_call x4, Pallas kernels, backward_layer(): pl.pallas_call(functools.partial(backward_kernel, down_steps, base, local...  94.7 us
    pallas_call x5, Pallas kernels, forward_layer(): pl.pallas_call(functools.partial(forward_kernel, up_steps, turn, base, lo...  91.2 us
    pallas_call x2, Pallas kernels, densify(): pl.pallas_call(functools.partial(densify_kernel, slots, step_slots), grid...  81.9 us
    ppermute x7, waiting for transfers between devices, shards(): current = lax.ppermute(send, 'section', pairs)  27.4 us
    ppermute x8, waiting for transfers between devices, other_core(): lax.ppermute(array, 'tp', [(index, index ^ 1) for index in range(lax.axis...  20.9 us
  transfers between devices with their start and end apart: 34, of which 27 were waited for; matrix products, arithmetic and copies ran while one was open for 2% of the time, Pallas kernels for 18%

commit v1 on v0

--- a/solution.py
+++ b/solution.py
@@ -168,7 +168,7 @@
     cols = right.shape[1]
     slots = block_index.shape[0]
     step_slots = slot_step(slots)
-    strip = min(rows, 1024 if rows > cols else STRIP)
+    strip = min(rows, 1024)
     strips = rows // strip
     return pl.pallas_call(
         functools.partial(block_grads_kernel, strips, step_slots),

time: 1030 us -> 1020 us (level)
  Pallas kernels: 370 us -> 354 us
    pallas_call x2, Pallas kernels: 102 us -> 85.9 us  [block_grads(): pl.pallas_call(functools.partial(block_grads_kernel, strips, step_slots),...]
  transfers between devices with their start and end apart: 34 -> 34, of which waited for: 27 -> 27; matrix products, arithmetic and copies ran while one was open for 2% -> 2% of each run, Pallas kernels for 18% -> 17%
where the time goes in v1:
time: 1020 us; the launch traced here: 1000 us
  waiting for transfers between devices  556 us (55%)
  Pallas kernels  354 us (35%)
  other arithmetic  52 us (5%)
  between operations  16.4 us (2%)
  starting transfers between devices  14.9 us (1%)
  local copies, waits for them, and re-layouts  10.7 us (1%)
    reduce_scatter x8, waiting for transfers between devices, row_sums(): lax.psum_scatter(chip, 'tp', scatter_dimension=0, tiled=True, axis_index_...  284 us
    all_gather x10, waiting for transfers between devices, all_rows(): return lax.all_gather(local_rows, 'tp', axis=0, tiled=True)  222 us
    pallas_call x4, Pallas kernels, backward_layer(): pl.pallas_call(functools.partial(backward_kernel, down_steps, base, local...  94.7 us
    pallas_call x5, Pallas kernels, forward_layer(): pl.pallas_call(functools.partial(forward_kernel, up_steps, turn, base, lo...  91.2 us
    pallas_call x2, Pallas kernels, block_grads(): pl.pallas_call(functools.partial(block_grads_kernel, strips, step_slots),...  85.9 us
    pallas_call x2, Pallas kernels, densify(): pl.pallas_call(functools.partial(densify_kernel, slots, step_slots), grid...  81.9 us
    ppermute x7, waiting for transfers between devices, shards(): current = lax.ppermute(send, 'section', pairs)  27.4 us
    ppermute x8, waiting for transfers between devices, other_core(): lax.ppermute(array, 'tp', [(index, index ^ 1) for index in range(lax.axis...  20.9 us
  transfers between devices with their start and end apart: 34, of which 27 were waited for; matrix products, arithmetic and copies ran while one was open for 2% of the time, Pallas kernels for 17%

profile of v1, /device:TPU:0, one launch (start us, length us, event | category | flops | bytes accessed | tf_op | source)
XLA Modules:
  0.0 1004.1 jit_solution(4365668573608322942)
XLA Ops:
  16.5 41.0 %densify.3.rest_1_.rest_0_ = bf16[2048,8192]{1,0:T(8,128)(2,1)} custom-call(s32[2304]{0:T(1024)} %fusion.62.index_ref, s32[1]{0:T(128)} %bitcast.87.count_ref, bf16[2304,4096]{1,0:T(8,128)(2,1)} %bitcast.89), custom_call_target="tpu_custom_call" | custom-call | tf_op jit(solution)/shard_map/densify/pallas_call | solution.py:102
  57.5 40.9 %densify.2.rest_0_.rest_1_ = bf16[8192,2048]{1,0:T(8,128)(2,1)} custom-call(s32[2304]{0:T(1024)} %reduce.index_ref, s32[1]{0:T(128)} %bitcast.85.count_ref, bf16[2304,4096]{1,0:T(8,128)(2,1)} %bitcast.90), custom_call_target="tpu_custom_call" | custom-call | tf_op jit(solution)/shard_map/densify/pallas_call | solution.py:102
  99.1 5.4 all-gather.29.cloned.1.call-done
  104.5 31.7 %forward_layer.5 = (bf16[64,8192]{1,0:T(8,128)(2,1)}, bf16[64,8192]{1,0:T(8,128)(2,1)}, bf16[384,8192]{1,0:T(8,128)(2,1)}, f32[384,2048]{1,0:T(8,128)}, bf16[384,2048]{1,0:T(8,128)(2,1)S(1)}) custom-call(s32[56]{0:T(128)} %stack.334.flags, bf16[128,8192]{1,0:T(8,128)(2,1)} %all-gather.13.cloned.1.call-done.rows_ref, ...), custom_call_target="tpu_custom_call" | custom-call | flops 8589934592 | bytes 67108864 | tf_op jit(solution)/shard_map/forward_layer/pallas_call | solution.py:354
  141.7 24.9 %reduce-scatter.10.cloned.1.call-done = bf16[16,8192]{1,0:T(8,128)(2,1)} async-done(((bf16[64,8192]{1,0:T(8,128)(2,1)}), bf16[16,8192]{1,0:T(8,128)(2,1)}) %reduce-scatter.10.cloned.1.call-update) | async-done | bytes 262160 | tf_op jit(solution)/shard_map/reduce_scatter | solution.py:222
  172.2 5.3 collective-permute-done.1
  178.7 6.1 maximum_maximum_fusion.rest_2_
  184.8 22.0 %all-gather.15.cloned.1.call-done.rows_ref = bf16[128,8192]{1,0:T(8,128)(2,1)} async-done(((bf16[16,8192]{1,0:T(8,128)(2,1)}), bf16[128,8192]{1,0:T(8,128)(2,1)}) %all-gather.15.cloned.1.call-update) | async-done | bytes 2097168 | tf_op jit(solution)/shard_map/all_gather | solution.py:217
  206.8 31.7 %forward_layer.6 = (bf16[64,8192]{1,0:T(8,128)(2,1)}, bf16[64,8192]{1,0:T(8,128)(2,1)}, bf16[384,8192]{1,0:T(8,128)(2,1)}, f32[384,2048]{1,0:T(8,128)}, bf16[384,2048]{1,0:T(8,128)(2,1)S(1)}) custom-call(s32[56]{0:T(128)} %stack.334.flags, ...), custom_call_target="tpu_custom_call", output_to_operand_aliasing={{2}: (4, {}), {3}: (5, {}), {4}: (6, {})} | custom-call | flops 8589934592 | bytes 67108864 | tf_op jit(solution)/shard_map/forward_layer/pallas_call | solution.py:354
  245.6 24.2 %reduce-scatter.12.cloned.1.call-done = bf16[16,8192]{1,0:T(8,128)(2,1)} async-done(((bf16[64,8192]{1,0:T(8,128)(2,1)}), bf16[16,8192]{1,0:T(8,128)(2,1)}) %reduce-scatter.12.cloned.1.call-update) | async-done | bytes 262160 | tf_op jit(solution)/shard_map/reduce_scatter | solution.py:222
  280.8 29.1 %all-gather.17.cloned.1.call-done.rows_ref = bf16[128,8192]{1,0:T(8,128)(2,1)} async-done(((bf16[16,8192]{1,0:T(8,128)(2,1)}), bf16[128,8192]{1,0:T(8,128)(2,1)}) %all-gather.17.cloned.1.call-update) | async-done | bytes 2097168 | tf_op jit(solution)/shard_map/all_gather | solution.py:217
  309.8 8.9 forward_layer.7
  324.2 48.7 %reduce-scatter.14.cloned.1.call-done = bf16[16,8192]{1,0:T(8,128)(2,1)} async-done(((bf16[64,8192]{1,0:T(8,128)(2,1)}), bf16[16,8192]{1,0:T(8,128)(2,1)}) %reduce-scatter.14.cloned.1.call-update) | async-done | bytes 262160 | tf_op jit(solution)/shard_map/reduce_scatter | solution.py:222
  375.7 37.1 %all-gather.19.cloned.1.call-done.rows_ref = bf16[128,8192]{1,0:T(8,128)(2,1)} async-done(((bf16[16,8192]{1,0:T(8,128)(2,1)}), bf16[128,8192]{1,0:T(8,128)(2,1)}) %all-gather.19.cloned.1.call-update) | async-done | bytes 2097168 | tf_op jit(solution)/shard_map/all_gather | solution.py:217
  412.8 9.4 forward_layer.8
  427.8 53.2 %reduce-scatter.16.cloned.1.call-done = bf16[16,8192]{1,0:T(8,128)(2,1)} async-done(((bf16[64,8192]{1,0:T(8,128)(2,1)}), bf16[16,8192]{1,0:T(8,128)(2,1)}) %reduce-scatter.16.cloned.1.call-update) | async-done | bytes 262160 | tf_op jit(solution)/shard_map/reduce_scatter | solution.py:222
  486.5 37.1 %all-gather.21.cloned.1.call-done.rows_ref.grad_ref = bf16[128,8192]{1,0:T(8,128)(2,1)} async-done(((bf16[16,8192]{1,0:T(8,128)(2,1)}), bf16[128,8192]{1,0:T(8,128)(2,1)}) %all-gather.21.cloned.1.call-update) | async-done | bytes 2097168 | tf_op jit(solution)/shard_map/all_gather | solution.py:217
  523.6 9.4 forward_layer.9
  533.1 9.1 backward_layer.4
  547.9 54.9 %reduce-scatter.18.cloned.1.call-done = bf16[16,8192]{1,0:T(8,128)(2,1)} async-done(((bf16[64,8192]{1,0:T(8,128)(2,1)}), bf16[16,8192]{1,0:T(8,128)(2,1)}) %reduce-scatter.18.cloned.1.call-update) | async-done | bytes 262160 | tf_op jit(solution)/shard_map/reduce_scatter | solution.py:222
  607.0 37.1 %all-gather.23.cloned.1.call-done.grad_ref = bf16[128,8192]{1,0:T(8,128)(2,1)} async-done(((bf16[16,8192]{1,0:T(8,128)(2,1)}), bf16[128,8192]{1,0:T(8,128)(2,1)}) %all-gather.23.cloned.1.call-update) | async-done | bytes 2097168 | tf_op jit(solution)/shard_map/all_gather | solution.py:217
  644.1 9.0 backward_layer.5
  661.4 52.2 %reduce-scatter.20.cloned.1.call-done = bf16[16,8192]{1,0:T(8,128)(2,1)} async-done(((bf16[64,8192]{1,0:T(8,128)(2,1)}), bf16[16,8192]{1,0:T(8,128)(2,1)}) %reduce-scatter.20.cloned.1.call-update) | async-done | bytes 262160 | tf_op jit(solution)/shard_map/reduce_scatter | solution.py:222
  716.3 8.5 collective-permute-done.11
  725.6 28.0 %all-gather.25.cloned.1.call-done.grad_ref = bf16[128,8192]{1,0:T(8,128)(2,1)} async-done(((bf16[16,8192]{1,0:T(8,128)(2,1)}), bf16[128,8192]{1,0:T(8,128)(2,1)}) %all-gather.25.cloned.1.call-update) | async-done | bytes 2097168 | tf_op jit(solution)/shard_map/all_gather | solution.py:217
  753.6 38.2 %backward_layer.6 = (bf16[64,8192]{1,0:T(8,128)(2,1)}, bf16[64,8192]{1,0:T(8,128)(2,1)}, bf16[384,8192]{1,0:T(8,128)(2,1)}, bf16[384,2048]{1,0:T(8,128)(2,1)}) custom-call(s32[56]{0:T(128)} %stack.334.flags, bf16[128,8192]{1,0:T(8,128)(2,1)} %all-gather.25.cloned.1.call-done.grad_ref, ...), custom_call_target="tpu_custom_call", output_to_operand_aliasing={{2}: (5, {}), {3}: (6, {})} | custom-call | flops 8589934592 | bytes 67108864 | tf_op jit(solution)/shard_map/backward_layer/pallas_call | solution.py:447
  797.4 25.8 %reduce-scatter.22.cloned.1.call-done = bf16[16,8192]{1,0:T(8,128)(2,1)} async-done(((bf16[64,8192]{1,0:T(8,128)(2,1)}), bf16[16,8192]{1,0:T(8,128)(2,1)}) %reduce-scatter.22.cloned.1.call-update) | async-done | bytes 262160 | tf_op jit(solution)/shard_map/reduce_scatter | solution.py:222
  826.9 8.5 collective-permute-done.13
  836.1 26.3 %all-gather.27.cloned.1.call-done.grad_ref = bf16[128,8192]{1,0:T(8,128)(2,1)} async-done(((bf16[16,8192]{1,0:T(8,128)(2,1)}), bf16[128,8192]{1,0:T(8,128)(2,1)}) %all-gather.27.cloned.1.call-update) | async-done | bytes 2097168 | tf_op jit(solution)/shard_map/all_gather | solution.py:217
  862.4 38.3 %backward_layer.7 = (bf16[64,8192]{1,0:T(8,128)(2,1)}, bf16[64,8192]{1,0:T(8,128)(2,1)}, bf16[384,8192]{1,0:T(8,128)(2,1)}, bf16[384,2048]{1,0:T(8,128)(2,1)}) custom-call(s32[56]{0:T(128)} %stack.334.flags, bf16[128,8192]{1,0:T(8,128)(2,1)} %all-gather.27.cloned.1.call-done.grad_ref, ...), custom_call_target="tpu_custom_call", output_to_operand_aliasing={{2}: (5, {}), {3}: (6, {})} | custom-call | flops 8589934592 | bytes 67108864 | tf_op jit(solution)/shard_map/backward_layer/pallas_call | solution.py:447
  906.8 42.7 %block_grads.3 = bf16[2304,4096]{1,0:T(8,128)(2,1)} custom-call(s32[2304]{0:T(1024)} %copy-done.15, s32[1]{0:T(128)} %bitcast.88.count_ref, bf16[384,2048]{1,0:T(8,128)(2,1)S(1)} %get-tuple-element.138.left_ref, bf16[384,8192]{1,0:T(8,128)(2,1)} %get-tuple-element.157.right_ref), custom_call_target="tpu_custom_call" | custom-call | flops 25769803776 | bytes 100663296 | tf_op jit(solution)/shard_map/block_grads/pallas_call | solution.py:173
  949.5 43.2 %block_grads.2 = bf16[2304,4096]{1,0:T(8,128)(2,1)} custom-call(s32[2304]{0:T(1024)} %reduce.index_ref, s32[1]{0:T(128)} %bitcast.86.count_ref, bf16[384,8192]{1,0:T(8,128)(2,1)} %get-tuple-element.153.left_ref, bf16[384,2048]{1,0:T(8,128)(2,1)} %get-tuple-element.154.right_ref), custom_call_target="tpu_custom_call" | custom-call | flops 25769803776 | bytes 100663296 | tf_op jit(solution)/shard_map/block_grads/pallas_call | solution.py:173
  (175 shorter events, 103.5 us)
Async XLA Ops:
  7.2 91.9 %all-gather.13.cloned.1.call-start = ((), (), s32[]{:S(2)}) async-start(), calls=%async_computation.9 | async-start | bytes 2359296 | tf_op jit(solution)/shard_map/all_gather | solution.py:217
  11.0 88.1 %all-gather.31.cloned.1.call-start = ((), (), s32[]{:S(2)}) async-start(), calls=%async_computation.27 | async-start | bytes 2359296 | tf_op jit(solution)/shard_map/all_gather | solution.py:217
  12.9 91.6 %all-gather.29.cloned.1.call-start = ((), (), s32[]{:S(2)}) async-start(), calls=%async_computation.26 | async-start | bytes 2359296 | tf_op jit(solution)/shard_map/all_gather | solution.py:217
  13.6 153.0 %reduce-scatter.10.cloned.1.call-start = ((), (), s32[]{:S(2)}) async-start(), calls=%async_computation.10 | async-start | bytes 1310720 | tf_op jit(solution)/shard_map/reduce_scatter | solution.py:222
  136.3 2.9 collective-permute-start
  141.7 65.1 %all-gather.15.cloned.1.call-start = ((), (), s32[]{:S(2)}) async-start(), calls=%async_computation.11 | async-start | bytes 2359296 | tf_op jit(solution)/shard_map/all_gather | solution.py:217
  168.7 8.7 collective-permute-start.1
  178.6 91.2 %reduce-scatter.12.cloned.1.call-start = ((), (), s32[]{:S(2)}) async-start(), calls=%async_computation.12 | async-start | bytes 1310720 | tf_op jit(solution)/shard_map/reduce_scatter | solution.py:222
  238.5 2.9 collective-permute-start.2
  243.9 65.9 %all-gather.17.cloned.1.call-start = ((), (), s32[]{:S(2)}) async-start(), calls=%async_computation.13 | async-start | bytes 2359296 | tf_op jit(solution)/shard_map/all_gather | solution.py:217
  270.9 8.8 collective-permute-start.3
  280.7 92.2 %reduce-scatter.14.cloned.1.call-start = ((), (), s32[]{:S(2)}) async-start(), calls=%async_computation.14 | async-start | bytes 1310720 | tf_op jit(solution)/shard_map/reduce_scatter | solution.py:222
  318.7 2.9 collective-permute-start.4
  324.1 88.7 %all-gather.19.cloned.1.call-start = ((), (), s32[]{:S(2)}) async-start(), calls=%async_computation.15 | async-start | bytes 2359296 | tf_op jit(solution)/shard_map/all_gather | solution.py:217
  375.7 105.3 %reduce-scatter.16.cloned.1.call-start = ((), (), s32[]{:S(2)}) async-start(), calls=%async_computation.16 | async-start | bytes 1310720 | tf_op jit(solution)/shard_map/reduce_scatter | solution.py:222
  422.3 2.9 collective-permute-start.6
  427.7 95.9 %all-gather.21.cloned.1.call-start = ((), (), s32[]{:S(2)}) async-start(), calls=%async_computation.17 | async-start | bytes 2359296 | tf_op jit(solution)/shard_map/all_gather | solution.py:217
  486.2 116.6 %reduce-scatter.18.cloned.1.call-start = ((), (), s32[]{:S(2)}) async-start(), calls=%async_computation.18 | async-start | bytes 1310720 | tf_op jit(solution)/shard_map/reduce_scatter | solution.py:222
  543.7 2.7 collective-permute-start.8
  547.8 96.3 %all-gather.23.cloned.1.call-start = ((), (), s32[]{:S(2)}) async-start(), calls=%async_computation.19 | async-start | bytes 2359296 | tf_op jit(solution)/shard_map/all_gather | solution.py:217
  605.5 0.7 collective-permute-start.9
  607.0 106.6 %reduce-scatter.20.cloned.1.call-start = ((), (), s32[]{:S(2)}) async-start(), calls=%async_computation.20 | async-start | bytes 1310720 | tf_op jit(solution)/shard_map/reduce_scatter | solution.py:222
  653.2 2.9 collective-permute-start.10
  658.6 95.0 %all-gather.25.cloned.1.call-start = ((), (), s32[]{:S(2)}) async-start(), calls=%async_computation.21 | async-start | bytes 2359296 | tf_op jit(solution)/shard_map/all_gather | solution.py:217
  715.0 9.8 collective-permute-start.11
  725.6 97.7 %reduce-scatter.22.cloned.1.call-start = ((), (), s32[]{:S(2)}) async-start(), calls=%async_computation.22 | async-start | bytes 1310720 | tf_op jit(solution)/shard_map/reduce_scatter | solution.py:222
  791.9 2.9 collective-permute-start.12
  797.3 65.0 %all-gather.27.cloned.1.call-start = ((), (), s32[]{:S(2)}) async-start(), calls=%async_computation.23 | async-start | bytes 2359296 | tf_op jit(solution)/shard_map/all_gather | solution.py:217
  825.6 9.8 collective-permute-start.13
  836.1 156.6 %reduce-scatter.26.cloned.1.call-start = ((), (), s32[]{:S(2)}) async-start(), calls=%async_computation.25 | async-start | bytes 1310720 | tf_op jit(solution)/shard_map/reduce_scatter | solution.py:222
  900.6 2.9 collective-permute-start.14
  906.1 89.0 %reduce-scatter.24.cloned.1.call-start = ((), (), s32[]{:S(2)}) async-start(), calls=%async_computation.24 | async-start | bytes 4718592 | tf_op jit(solution)/shard_map/reduce_scatter | solution.py:539
  (20 other events, 321.1 us)
Sparse Core Ops, SparseCore 0:
  11.1 31.7 all-gather.12
  45.1 28.5 all-gather.30
  75.9 28.5 all-gather.28
  141.8 24.8 reduce-scatter.9
  178.7 28.0 all-gather.14
  244.1 25.6 reduce-scatter.11
  280.8 28.9 all-gather.16
  324.3 48.5 reduce-scatter.13
  375.8 37.0 all-gather.18
  427.8 53.0 reduce-scatter.15
  486.4 37.2 all-gather.20
  548.0 54.8 reduce-scatter.17
  607.1 37.0 all-gather.22
  658.8 54.8 reduce-scatter.19
  725.7 27.9 all-gather.24
  797.5 25.7 reduce-scatter.21
  836.2 26.1 all-gather.26
  906.2 24.8 reduce-scatter.25
  933.4 48.6 reduce-scatter.23
